TPU v7x, 32 devices: a whole 2x2x4 slice. The times are simulated.
32 devices in a mesh: dp: 16 (over z, y, x), pipe: 2 (over core).
Axes of the slice: x: 2, y: 2, z: 4, core: 2. Of those that a mesh axis runs over, the one named last changes fastest.
Arguments:
- enc_tokens: bfloat16 [2, 1536, 2048], P(None, 'dp'), may hold values from -6 to 6
- dec_tokens: bfloat16 [2, 512, 2048], P(None, 'dp'), may hold values from -6 to 6
- enc_segments: int32 [2, 1536], P(None, 'dp'), may hold values from 0 to 3, as said below
- dec_segments: int32 [2, 512], P(None, 'dp'), may hold values from 0 to 3, as said below
- proj_in: bfloat16 [2, 3, 2048, 128], P('pipe'), may hold values from -0.125 to 0.125
- proj_out: bfloat16 [2, 128, 2048], P('pipe'), may hold values from -0.5 to 0.5
- cotangent: bfloat16 [2, 512, 2048], P(None, 'dp'), may hold values from -6 to 6
Outputs:
- grad_in: float32 [2, 3, 2048, 128], P('pipe', None, 'dp')
- grad_out: float32 [2, 128, 2048], P('pipe', None, 'dp')
Inputs may be any that keep to these rules, and one draw needn't show every extreme that they name: `enc_segments`: in each microbatch and each aligned block of 96 encoder rows the ids start at 0, never fall, rise by at most one from row to row and end at 3; equal ids are one packed sample. `dec_segments`: decoder row j of a block carries the id of encoder row (j * 96) // 32 of the same block and microbatch, so every decoder token's sample has encoder tokens.
All inputs are finite; a program needn't handle non-finite values.
Results may differ from a plain program's by a relative error of at most 0.012.
Values may be sent and summed in bfloat16 or wider, within the bound.
A program may use at most 64 MiB of HBM per device.

v0:
```python
import math

import jax
import jax.numpy as jnp
from jax import lax
from jax.sharding import PartitionSpec as P


def shifted(value, axis, by):
    length = lax.axis_size(axis)
    pairs = [(i, i + by) for i in range(length) if 0 <= i + by < length]
    return lax.ppermute(value, axis, pairs)


def normalize(values):
    return values * lax.rsqrt(jnp.mean(values * values, axis=-1, keepdims=True) + 1e-06)


def attention(queries, key_rows, value_rows, allowed):
    scores = jnp.dot(queries, key_rows.T, preferred_element_type=jnp.float32) * (
        1.0 / math.sqrt(queries.shape[-1])
    )
    scores = jnp.where(allowed, scores, -1e30)
    row_max = jnp.max(scores, axis=-1, keepdims=True)
    expo = jnp.exp(scores - row_max)
    probabilities = (expo / jnp.sum(expo, axis=-1, keepdims=True)).astype(jnp.bfloat16)
    return jnp.dot(probabilities, value_rows, preferred_element_type=jnp.float32).astype(
        jnp.bfloat16
    )


def section_apply(weights_in, weights_out, buffer, enc_ids, dec_ids, encoder_layer):
    enc_count = enc_ids.shape[0]
    memory = buffer[:enc_count]
    stream = buffer[enc_count:]
    if encoder_layer:
        residual = memory.astype(jnp.float32)
        normalized = normalize(residual).astype(jnp.bfloat16)
        queries = jnp.dot(normalized, weights_in[0], preferred_element_type=jnp.float32).astype(
            jnp.bfloat16
        )
        key_rows = jnp.dot(normalized, weights_in[1], preferred_element_type=jnp.float32).astype(
            jnp.bfloat16
        )
        value_rows = jnp.dot(normalized, weights_in[2], preferred_element_type=jnp.float32).astype(
            jnp.bfloat16
        )
        allowed = enc_ids[:, None] == enc_ids[None, :]
        attended = attention(queries, key_rows, value_rows, allowed)
        updated = (
            residual + jnp.dot(attended, weights_out, preferred_element_type=jnp.float32)
        ).astype(jnp.bfloat16)
        return jnp.concatenate([updated, stream], axis=0)
    residual = stream.astype(jnp.float32)
    normalized = normalize(residual).astype(jnp.bfloat16)
    source = normalize(memory.astype(jnp.float32)).astype(jnp.bfloat16)
    queries = jnp.dot(normalized, weights_in[0], preferred_element_type=jnp.float32).astype(
        jnp.bfloat16
    )
    key_rows = jnp.dot(source, weights_in[1], preferred_element_type=jnp.float32).astype(
        jnp.bfloat16
    )
    value_rows = jnp.dot(source, weights_in[2], preferred_element_type=jnp.float32).astype(
        jnp.bfloat16
    )
    allowed = dec_ids[:, None] == enc_ids[None, :]
    attended = attention(queries, key_rows, value_rows, allowed)
    updated = (
        residual + jnp.dot(attended, weights_out, preferred_element_type=jnp.float32)
    ).astype(jnp.bfloat16)
    return jnp.concatenate([memory, updated], axis=0)


def pick_micro(array, micro_index):
    return lax.dynamic_index_in_dim(array, micro_index, 0, keepdims=False)


def body(enc_tokens, dec_tokens, enc_segments, dec_segments, proj_in, proj_out, cotangent):
    layer_count = lax.axis_size("pipe")
    position = lax.axis_index("pipe")
    micro_count, enc_count, model_width = enc_tokens.shape
    dec_count = dec_tokens.shape[1]
    row_count = enc_count + dec_count
    local_in = proj_in[0]
    local_out = proj_out[0]
    halfway = layer_count // 2

    def apply_layer(weights_in, weights_out, buffer, micro_index):
        enc_ids = pick_micro(enc_segments, micro_index)
        dec_ids = pick_micro(dec_segments, micro_index)

        def encoder_branch(operands):
            return section_apply(
                operands[0], operands[1], operands[2], operands[3], operands[4], True
            )

        def decoder_branch(operands):
            return section_apply(
                operands[0], operands[1], operands[2], operands[3], operands[4], False
            )

        return lax.cond(
            position < halfway,
            encoder_branch,
            decoder_branch,
            (weights_in, weights_out, buffer, enc_ids, dec_ids),
        )

    def forward_part(step_index, received, saved_inputs):
        micro_index = step_index - position
        active = (micro_index >= 0) & (micro_index < micro_count)
        clipped = jnp.clip(micro_index, 0, micro_count - 1)
        fresh_inputs = jnp.concatenate(
            [pick_micro(enc_tokens, clipped), pick_micro(dec_tokens, clipped)], axis=0
        )
        buffer = jnp.where(position == 0, fresh_inputs, received)

        def compute_layer():
            return apply_layer(local_in, local_out, buffer, clipped)

        def pass_along():
            return buffer

        result = lax.cond(active, compute_layer, pass_along)
        saved_inputs = jnp.where(
            active, lax.dynamic_update_index_in_dim(saved_inputs, buffer, clipped, 0), saved_inputs
        )
        received = shifted(result, "pipe", 1)
        return (received, saved_inputs)

    def backward_part(step_index, received, totals, saved_inputs):
        micro_index = step_index - (layer_count - 1 - position)
        active = (micro_index >= 0) & (micro_index < micro_count)
        clipped = jnp.clip(micro_index, 0, micro_count - 1)
        buffer = pick_micro(saved_inputs, clipped)
        start_rows = jnp.concatenate(
            [jnp.zeros((enc_count, model_width), jnp.bfloat16), pick_micro(cotangent, clipped)],
            axis=0,
        )
        incoming = jnp.where(position == layer_count - 1, start_rows, received)

        def layer_of(weights_in, weights_out, layer_input):
            return apply_layer(weights_in, weights_out, layer_input, clipped)

        def differentiate():
            result, pullback = jax.vjp(layer_of, local_in, local_out, buffer)
            grad_weights_in, grad_weights_out, grad_buffer = pullback(incoming)
            return (
                grad_weights_in.astype(jnp.float32),
                grad_weights_out.astype(jnp.float32),
                grad_buffer,
            )

        def nothing_due():
            return (
                jnp.zeros(local_in.shape, jnp.float32),
                jnp.zeros(local_out.shape, jnp.float32),
                jnp.zeros((row_count, model_width), jnp.bfloat16),
            )

        grad_weights_in, grad_weights_out, grad_buffer = lax.cond(
            active, differentiate, nothing_due
        )
        received = shifted(grad_buffer, "pipe", -1)
        return (received, (totals[0] + grad_weights_in, totals[1] + grad_weights_out))

    blank_buffer = jnp.zeros((row_count, model_width), jnp.bfloat16)
    saved_start = jnp.zeros((micro_count, row_count, model_width), jnp.bfloat16)
    totals_start = (jnp.zeros(local_in.shape, jnp.float32), jnp.zeros(local_out.shape, jnp.float32))

    def forward_loop(step_index, running):
        return forward_part(step_index, running[0], running[1])

    unused_buffer, saved_inputs = lax.fori_loop(
        0, micro_count + layer_count - 1, forward_loop, (blank_buffer, saved_start)
    )

    def backward_loop(step_index, running):
        return backward_part(step_index, running[0], running[1], saved_inputs)

    unused_rows, totals = lax.fori_loop(
        0, micro_count + layer_count - 1, backward_loop, (blank_buffer, totals_start)
    )
    summed_in, summed_out = (
        lax.psum_scatter(totals[0], "dp", scatter_dimension=1, tiled=True),
        lax.psum_scatter(totals[1], "dp", scatter_dimension=1, tiled=True),
    )
    return (summed_in[None], summed_out[None])


def solution(mesh):
    return jax.shard_map(
        body,
        mesh=mesh,
        in_specs=(
            P(None, "dp", None),
            P(None, "dp", None),
            P(None, "dp"),
            P(None, "dp"),
            P("pipe", None, None, None),
            P("pipe", None, None),
            P(None, "dp", None),
        ),
        out_specs=(P("pipe", None, "dp", None), P("pipe", None, "dp")),
        check_vma=False,
    )
```

profile of v0, /device:TPU:0, one launch (start us, length us, event | category | flops | bytes accessed | tf_op | source)
XLA Modules:
  0.0 338.4 jit_solution(1369525673108942980)
XLA Ops:
  8.5 34.8 %while.35 = (s32[]{:T(128)}, bf16[128,2048]{1,0:T(8,128)(2,1)S(1)}, bf16[2,128,2048]{2,1,0:T(8,128)(2,1)}, s32[]{:T(128)}, pred[]{:T(512)}, /*index=5*/bf16[2,96...) while((s32[]{:T(128)}, bf16[128,2048]{1,0:T(8,128)(2,1)S(1)}, ...), condition=%wide.region_12.13_spmd, body=%wide.region_0.12_spmd.sunk | while | flops 211747744 | bytes 18042580 | solution.py:174
  9.6 1.7 dynamic-slice_bitcast_fusion.9
  11.3 2.2 fusion.197
  13.5 2.5 conditional.14
  14.2 1.8 conditional.4
  17.3 1.5 collective-permute-done
  19.9 1.7 dynamic-slice_bitcast_fusion.9
  21.5 2.2 fusion.197
  23.8 2.5 conditional.14
  24.5 1.8 conditional.4
  26.3 3.2 collective-permute-start
  29.5 1.5 collective-permute-done
  32.1 1.7 dynamic-slice_bitcast_fusion.9
  33.8 2.2 fusion.197
  36.0 5.8 %collective-permute-start = (bf16[128,2048]{1,0:T(8,128)(2,1)S(1)}, bf16[128,2048]{1,0:T(8,128)(2,1)S(1)}, u32[]{:S(2)}, u32[]{:S(2)}) collective-permute-start(bf16[128,2048]{1,0:T(8,128)(2,1)S(1)} %get-tuple-element.1530), channel_id=1, source_target_pairs={{0,1},{2,3},{4,5},{6,7},{8,9},{10,11},{12,13},{14,15},{16,17},{18,... | collective-permute-start | bytes 1572872 | tf_op jit(solution)/shard_map/while/body/eval_jaxpr/ppermute | solution.py:12
  41.8 1.5 collective-permute-done
  43.3 123.0 %while.36 = (s32[]{:T(128)}, bf16[128,2048]{1,0:T(8,128)(2,1)S(1)}, f32[3,2048,128]{1,2,0:T(8,128)}, f32[128,2048]{1,0:T(8,128)}, s32[]{:T(128)}, /*index=5*/s32...) while((s32[]{:T(128)}, bf16[128,2048]{1,0:T(8,128)(2,1)S(1)}, ...), condition=%wide.region_36.37_spmd.clone, body=%wide.region_13.36_spmd.clone.sunk | while | flops 579561024 | bytes 70686472 | solution.py:181
  43.3 4.0 %conditional.15 = (f32[3,2048,128]{1,2,0:T(8,128)}, f32[128,2048]{1,0:T(8,128)}, bf16[128,2048]{1,0:T(8,128)(2,1)}) conditional(s32[]{:T(128)} %convert_element_type.540, () %tuple.200, (s32[]{:T(128)}, pred[]{:T(512)}, s32[]{:T(128)}, bf16[2,32,2048]{2,1,0:T(8,128)(2,1)}, bf16[128,2048]{1,0:T(8,128)(2,1)S(1)}, ...), branch_computations={%region_14.14_spmd, %region_15.35_spmd} | conditional | flops 577463872 | bytes 47617432 | solution.py:161
  43.4 2.1 broadcast.338
  48.7 4.4 %select_add_fusion.4 = f32[3,2048,128]{1,2,0:T(8,128)} fusion(f32[3,2048,128]{1,2,0:T(8,128)} %get-tuple-element.1361, f32[3,2048,128]{1,2,0:T(8,128)} %get-tuple-element.1499, pred[]{:T(512)S(6)} %compare.14), kind=kLoop, calls=%fused_computation.212.clone.1 | loop fusion | flops 1572864 | bytes 9437185 | tf_op jit(solution)/shard_map/while/body/eval_jaxpr/add | solution.py:165
  53.1 1.6 select_add_fusion.5
  54.7 22.5 %collective-permute-done.1 = bf16[128,2048]{1,0:T(8,128)(2,1)S(1)} collective-permute-done((bf16[128,2048]{1,0:T(8,128)(2,1)}, bf16[128,2048]{1,0:T(8,128)(2,1)S(1)}, u32[]{:S(2)}, u32[]{:S(2)}) %collective-permute-start.1) | collective-permute-done | bytes 524320 | tf_op jit(solution)/shard_map/while/body/eval_jaxpr/ppermute | solution.py:12
  77.2 35.3 %conditional.15 = (f32[3,2048,128]{1,2,0:T(8,128)}, f32[128,2048]{1,0:T(8,128)}, bf16[128,2048]{1,0:T(8,128)(2,1)}) conditional(s32[]{:T(128)} %convert_element_type.540, () %tuple.200, (s32[]{:T(128)}, pred[]{:T(512)}, s32[]{:T(128)}, bf16[2,32,2048]{2,1,0:T(8,128)(2,1)}, bf16[128,2048]{1,0:T(8,128)(2,1)S(1)}, ...), branch_computations={%region_14.14_spmd, %region_15.35_spmd} | conditional | flops 577463872 | bytes 47617432 | solution.py:161
  79.0 11.9 %conditional.10 = (f32[32,2048]{1,0:T(8,128)S(1)}, f32[32,1]{0,1:T(1,128)S(1)}, f32[32,1]{0,1:T(1,128)S(1)}, f32[96,1]{0,1:T(1,128)S(1)}, f32[96,1]{0,1:T(1,128)...) conditional(s32[]{:T(128)} %convert_element_type.327, ...), branch_computations={%region_16.20_spmd, %region_22.25_spmd} | conditional | flops 157041024 | bytes 17965564
  81.9 2.0 convolution_convert_fusion.12
  83.9 2.1 fusion.129
  87.0 2.0 convolution_convert_fusion.11
  92.6 17.8 %conditional.11 = (bf16[128,2048]{1,0:T(8,128)(2,1)}, f32[128,2048]{1,0:T(8,128)}, bf16[3,2048,128]{1,2,0:T(8,128)(2,1)S(1)}) conditional(s32[]{:T(128)} %convert_element_type.327, (bf16[128,2048]{1,0:T(8,128)(2,1)S(1)}, bf16[128,2048]{1,0:T(8,128)(2,1)S(1)}, bf16[96,128]{1,0:T(8,128)(2,1)}, f32[32,1]{0,1:T(1,128)S(1)}, f32[32,1]{0,1:T(1,128)S(1)}, ...), branch_computations={%region_27.30_spmd, %region_32.34_spmd} | conditional | flops 419177664 | bytes 17785280
  105.0 1.3 convolution_convert_fusion.29
  106.4 1.5 multiply_reduce_fusion.4
  110.4 2.1 convert_element_type.347
  113.8 5.4 %select_add_fusion.4 = f32[3,2048,128]{1,2,0:T(8,128)} fusion(f32[3,2048,128]{1,2,0:T(8,128)} %get-tuple-element.1361, f32[3,2048,128]{1,2,0:T(8,128)} %get-tuple-element.1499, pred[]{:T(512)S(6)} %compare.14), kind=kLoop, calls=%fused_computation.212.clone.1 | loop fusion | flops 1572864 | bytes 9437185 | tf_op jit(solution)/shard_map/while/body/eval_jaxpr/add | solution.py:165
  119.2 1.6 select_add_fusion.5
  121.8 35.3 %conditional.15 = (f32[3,2048,128]{1,2,0:T(8,128)}, f32[128,2048]{1,0:T(8,128)}, bf16[128,2048]{1,0:T(8,128)(2,1)}) conditional(s32[]{:T(128)} %convert_element_type.540, () %tuple.200, (s32[]{:T(128)}, pred[]{:T(512)}, s32[]{:T(128)}, bf16[2,32,2048]{2,1,0:T(8,128)(2,1)}, bf16[128,2048]{1,0:T(8,128)(2,1)S(1)}, ...), branch_computations={%region_14.14_spmd, %region_15.35_spmd} | conditional | flops 577463872 | bytes 47617432 | solution.py:161
  123.6 11.9 %conditional.10 = (f32[32,2048]{1,0:T(8,128)S(1)}, f32[32,1]{0,1:T(1,128)S(1)}, f32[32,1]{0,1:T(1,128)S(1)}, f32[96,1]{0,1:T(1,128)S(1)}, f32[96,1]{0,1:T(1,128)...) conditional(s32[]{:T(128)} %convert_element_type.327, ...), branch_computations={%region_16.20_spmd, %region_22.25_spmd} | conditional | flops 157041024 | bytes 17965564
  126.5 2.0 convolution_convert_fusion.12
  128.5 2.1 fusion.129
  131.6 2.0 convolution_convert_fusion.11
  137.2 17.8 %conditional.11 = (bf16[128,2048]{1,0:T(8,128)(2,1)}, f32[128,2048]{1,0:T(8,128)}, bf16[3,2048,128]{1,2,0:T(8,128)(2,1)S(1)}) conditional(s32[]{:T(128)} %convert_element_type.327, (bf16[128,2048]{1,0:T(8,128)(2,1)S(1)}, bf16[128,2048]{1,0:T(8,128)(2,1)S(1)}, bf16[96,128]{1,0:T(8,128)(2,1)}, f32[32,1]{0,1:T(1,128)S(1)}, f32[32,1]{0,1:T(1,128)S(1)}, ...), branch_computations={%region_27.30_spmd, %region_32.34_spmd} | conditional | flops 419177664 | bytes 17785280
  148.3 1.3 convolution_convert_fusion.30
  149.6 1.3 convolution_convert_fusion.29
  151.0 1.5 multiply_reduce_fusion.4
  155.0 2.1 convert_element_type.347
  158.4 5.4 %select_add_fusion.4 = f32[3,2048,128]{1,2,0:T(8,128)} fusion(f32[3,2048,128]{1,2,0:T(8,128)} %get-tuple-element.1361, f32[3,2048,128]{1,2,0:T(8,128)} %get-tuple-element.1499, pred[]{:T(512)S(6)} %compare.14), kind=kLoop, calls=%fused_computation.212.clone.1 | loop fusion | flops 1572864 | bytes 9437185 | tf_op jit(solution)/shard_map/while/body/eval_jaxpr/add | solution.py:165
  163.8 1.6 select_add_fusion.5
  166.4 3.6 %copy.22 = f32[3,2048,128]{2,1,0:T(8,128)} copy(f32[3,2048,128]{1,2,0:T(8,128)} %get-tuple-element.939) | data formatting | bytes 6291456 | tf_op jit(solution)/shard_map/while | solution.py:181
  170.0 77.7 %reduce-scatter.5.cloned.1.call-done = f32[128,128]{1,0:T(8,128)} async-done(((f32[128,2048]{1,0:T(8,128)}), f32[128,128]{1,0:T(8,128)}) %reduce-scatter.5.cloned.1.call-update) | async-done | bytes 65552 | tf_op jit(solution)/shard_map/reduce_scatter | solution.py:186
  247.8 83.8 %reduce-scatter.3.cloned.1.call-done = f32[3,128,128]{2,1,0:T(8,128)} async-done(((f32[3,2048,128]{2,1,0:T(8,128)}), f32[3,128,128]{2,1,0:T(8,128)}) %reduce-scatter.3.cloned.1.call-update) | async-done | bytes 196624 | tf_op jit(solution)/shard_map/reduce_scatter | solution.py:185
  (244 shorter events, 64.8 us)
Async XLA Ops:
  7.2 1.3 copy-start
  7.2 240.6 %reduce-scatter.5.cloned.1.call-start = ((), (), s32[]{:S(2)}) async-start(), calls=%async_computation.3 | async-start | bytes 1114112 | tf_op jit(solution)/shard_map/reduce_scatter | solution.py:186
  9.5 3.9 %copy-start.1 = (bf16[3,2048,128]{2,1,0:T(8,128)(2,1)S(1)}, bf16[3,2048,128]{2,1,0:T(8,128)(2,1)}, u32[]{:S(2)}) copy-start(bf16[3,2048,128]{2,1,0:T(8,128)(2,1)} %get-tuple-element.1476) | copy-start | bytes 4718596 | tf_op jit(solution)/shard_map/while
  16.0 2.8 collective-permute-start
  19.8 3.9 %copy-start.1 = (bf16[3,2048,128]{2,1,0:T(8,128)(2,1)S(1)}, bf16[3,2048,128]{2,1,0:T(8,128)(2,1)}, u32[]{:S(2)}) copy-start(bf16[3,2048,128]{2,1,0:T(8,128)(2,1)} %get-tuple-element.1476) | copy-start | bytes 4718596 | tf_op jit(solution)/shard_map/while
  26.3 4.7 %collective-permute-start = (bf16[128,2048]{1,0:T(8,128)(2,1)S(1)}, bf16[128,2048]{1,0:T(8,128)(2,1)S(1)}, u32[]{:S(2)}, u32[]{:S(2)}) collective-permute-start(bf16[128,2048]{1,0:T(8,128)(2,1)S(1)} %get-tuple-element.1530), channel_id=1, source_target_pairs={{0,1},{2,3},{4,5},{6,7},{8,9},{10,11},{12,13},{14,15},{16,17},{18,... | collective-permute-start | bytes 1572872 | tf_op jit(solution)/shard_map/while/body/eval_jaxpr/ppermute | solution.py:12
  32.1 3.9 %copy-start.1 = (bf16[3,2048,128]{2,1,0:T(8,128)(2,1)S(1)}, bf16[3,2048,128]{2,1,0:T(8,128)(2,1)}, u32[]{:S(2)}) copy-start(bf16[3,2048,128]{2,1,0:T(8,128)(2,1)} %get-tuple-element.1476) | copy-start | bytes 4718596 | tf_op jit(solution)/shard_map/while
  36.0 7.3 %collective-permute-start = (bf16[128,2048]{1,0:T(8,128)(2,1)S(1)}, bf16[128,2048]{1,0:T(8,128)(2,1)S(1)}, u32[]{:S(2)}, u32[]{:S(2)}) collective-permute-start(bf16[128,2048]{1,0:T(8,128)(2,1)S(1)} %get-tuple-element.1530), channel_id=1, source_target_pairs={{0,1},{2,3},{4,5},{6,7},{8,9},{10,11},{12,13},{14,15},{16,17},{18,... | collective-permute-start | bytes 1572872 | tf_op jit(solution)/shard_map/while/body/eval_jaxpr/ppermute | solution.py:12
  47.4 29.8 %collective-permute-start.1 = (bf16[128,2048]{1,0:T(8,128)(2,1)}, bf16[128,2048]{1,0:T(8,128)(2,1)S(1)}, u32[]{:S(2)}, u32[]{:S(2)}) collective-permute-start(bf16[128,2048]{1,0:T(8,128)(2,1)} %get-tuple-element.1360), channel_id=1, source_target_pairs={{1,0},{3,2},{5,4},{7,6},{9,8},{11,10},{13,12},{15,14},{17,16},{19,... | collective-permute-start | bytes 1572872 | tf_op jit(solution)/shard_map/while/body/eval_jaxpr/ppermute | solution.py:12
  48.7 4.5 %copy-start.8 = (f32[128,2048]{1,0:T(8,128)S(1)}, f32[128,2048]{1,0:T(8,128)}, u32[]{:S(2)}) copy-start(f32[128,2048]{1,0:T(8,128)} %get-tuple-element.1500) | copy-start | bytes 3145732 | tf_op jit(solution)/shard_map/while
  54.7 22.5 %copy-start.9 = (f32[128,2048]{1,0:T(8,128)}, f32[128,2048]{1,0:T(8,128)S(1)}, u32[]{:S(2)}) copy-start(f32[128,2048]{1,0:T(8,128)S(1)} %select_add_fusion.5) | copy-start | bytes 3145732 | tf_op jit(solution)/shard_map/while
  77.2 15.0 %copy-start.16 = (bf16[2,32,2048]{2,1,0:T(8,128)(2,1)S(1)}, bf16[2,32,2048]{2,1,0:T(8,128)(2,1)}, u32[]{:S(2)}) copy-start(bf16[2,32,2048]{2,1,0:T(8,128)(2,1)} %get-tuple-element.873) | copy-start | bytes 786436 | tf_op jit(solution)/shard_map/while/body/eval_jaxpr/cond
  79.0 1.7 copy-start.3
  79.2 2.7 copy-start.4
  83.9 6.9 %copy-start.5 = (bf16[96,2048]{1,0:T(8,128)(2,1)S(1)}, bf16[96,2048]{1,0:T(8,128)(2,1)}, u32[]{:S(2)}) copy-start(bf16[96,2048]{1,0:T(8,128)(2,1)} %copy-done.4) | copy-start | bytes 1179652
  90.9 0.7 copy-start.6
  91.6 0.6 copy-start.13
  91.6 0.7 copy-start.10
  91.6 0.7 copy-start.17
  91.6 1.0 copy-start.7
  92.6 9.4 %copy-start.14 = (bf16[96,128]{1,0:T(8,128)(2,1)}, bf16[96,128]{1,0:T(8,128)(2,1)S(1)}, u32[]{:S(2)}) copy-start(bf16[96,128]{1,0:T(8,128)(2,1)S(1)} %get-tuple-element.869) | copy-start | bytes 73732
  92.6 9.4 %copy-start.23 = (f32[96,1]{0,1:T(1,128)}, f32[96,1]{0,1:T(1,128)S(1)}, u32[]{:S(2)}) copy-start(f32[96,1]{0,1:T(1,128)S(1)} %get-tuple-element.866) | copy-start | bytes 1156
  92.6 9.4 %copy-start.29 = (f32[96,1]{0,1:T(1,128)}, f32[96,1]{0,1:T(1,128)S(1)}, u32[]{:S(2)}) copy-start(f32[96,1]{0,1:T(1,128)S(1)} %get-tuple-element.868) | copy-start | bytes 1156
  106.4 1.5 copy-start.30
  106.4 1.5 copy-start.24
  107.9 1.2 copy-start.15
  112.5 8.3 %collective-permute-start.1 = (bf16[128,2048]{1,0:T(8,128)(2,1)}, bf16[128,2048]{1,0:T(8,128)(2,1)S(1)}, u32[]{:S(2)}, u32[]{:S(2)}) collective-permute-start(bf16[128,2048]{1,0:T(8,128)(2,1)} %get-tuple-element.1360), channel_id=1, source_target_pairs={{1,0},{3,2},{5,4},{7,6},{9,8},{11,10},{13,12},{15,14},{17,16},{19,... | collective-permute-start | bytes 1572872 | tf_op jit(solution)/shard_map/while/body/eval_jaxpr/ppermute | solution.py:12
  113.8 5.4 %copy-start.8 = (f32[128,2048]{1,0:T(8,128)S(1)}, f32[128,2048]{1,0:T(8,128)}, u32[]{:S(2)}) copy-start(f32[128,2048]{1,0:T(8,128)} %get-tuple-element.1500) | copy-start | bytes 3145732 | tf_op jit(solution)/shard_map/while
  120.8 1.0 copy-start.9
  121.8 15.0 %copy-start.16 = (bf16[2,32,2048]{2,1,0:T(8,128)(2,1)S(1)}, bf16[2,32,2048]{2,1,0:T(8,128)(2,1)}, u32[]{:S(2)}) copy-start(bf16[2,32,2048]{2,1,0:T(8,128)(2,1)} %get-tuple-element.873) | copy-start | bytes 786436 | tf_op jit(solution)/shard_map/while/body/eval_jaxpr/cond
  123.6 1.7 copy-start.3
  123.8 2.7 copy-start.4
  128.5 6.9 %copy-start.5 = (bf16[96,2048]{1,0:T(8,128)(2,1)S(1)}, bf16[96,2048]{1,0:T(8,128)(2,1)}, u32[]{:S(2)}) copy-start(bf16[96,2048]{1,0:T(8,128)(2,1)} %copy-done.4) | copy-start | bytes 1179652
  135.5 0.7 copy-start.6
  136.2 0.6 copy-start.13
  136.2 0.7 copy-start.10
  136.2 0.7 copy-start.17
  136.2 1.0 copy-start.7
  137.2 9.4 %copy-start.14 = (bf16[96,128]{1,0:T(8,128)(2,1)}, bf16[96,128]{1,0:T(8,128)(2,1)S(1)}, u32[]{:S(2)}) copy-start(bf16[96,128]{1,0:T(8,128)(2,1)S(1)} %get-tuple-element.869) | copy-start | bytes 73732
  137.2 9.4 %copy-start.23 = (f32[96,1]{0,1:T(1,128)}, f32[96,1]{0,1:T(1,128)S(1)}, u32[]{:S(2)}) copy-start(f32[96,1]{0,1:T(1,128)S(1)} %get-tuple-element.866) | copy-start | bytes 1156
  137.2 9.4 %copy-start.29 = (f32[96,1]{0,1:T(1,128)}, f32[96,1]{0,1:T(1,128)S(1)}, u32[]{:S(2)}) copy-start(f32[96,1]{0,1:T(1,128)S(1)} %get-tuple-element.868) | copy-start | bytes 1156
  151.0 1.5 copy-start.30
  151.0 1.5 copy-start.24
  152.5 1.2 copy-start.15
  157.1 8.3 %collective-permute-start.1 = (bf16[128,2048]{1,0:T(8,128)(2,1)}, bf16[128,2048]{1,0:T(8,128)(2,1)S(1)}, u32[]{:S(2)}, u32[]{:S(2)}) collective-permute-start(bf16[128,2048]{1,0:T(8,128)(2,1)} %get-tuple-element.1360), channel_id=1, source_target_pairs={{1,0},{3,2},{5,4},{7,6},{9,8},{11,10},{13,12},{15,14},{17,16},{19,... | collective-permute-start | bytes 1572872 | tf_op jit(solution)/shard_map/while/body/eval_jaxpr/ppermute | solution.py:12
  158.4 5.4 %copy-start.8 = (f32[128,2048]{1,0:T(8,128)S(1)}, f32[128,2048]{1,0:T(8,128)}, u32[]{:S(2)}) copy-start(f32[128,2048]{1,0:T(8,128)} %get-tuple-element.1500) | copy-start | bytes 3145732 | tf_op jit(solution)/shard_map/while
  165.3 1.0 copy-start.9
  166.4 165.2 %reduce-scatter.3.cloned.1.call-start = ((), (), s32[]{:S(2)}) async-start(), calls=%async_computation.2 | async-start | bytes 3342336 | tf_op jit(solution)/shard_map/reduce_scatter | solution.py:185
  (4 other events, 2.5 us)
Sparse Core Ops, SparseCore 0:
  166.5 81.2 reduce-scatter.4
  250.7 80.7 reduce-scatter.2
where the time goes:
time: 341 us; the launch traced here: 338 us
  waiting for transfers between devices  188 us (55%)
  matrix products  44.4 us (13%)
  local copies, waits for them, and re-layouts  39.2 us (11%)
  other arithmetic  36.7 us (11%)
  starting transfers between devices  14.2 us (4%)
  between operations  14.1 us (4%)
    reduce_scatter x1, waiting for transfers between devices, body(): lax.psum_scatter(totals[0], 'dp', scatter_dimension=1, tiled=True)  83.8 us
    reduce_scatter x1, waiting for transfers between devices, body(): lax.psum_scatter(totals[1], 'dp', scatter_dimension=1, tiled=True)  77.7 us
    ppermute x6, waiting for transfers between devices, shifted(): return lax.ppermute(value, axis, pairs)  26.9 us
    add x3, other arithmetic, backward_part(): totals[0] + grad_weights_in  15.2 us
    ppermute x6, starting transfers between devices, shifted(): return lax.ppermute(value, axis, pairs)  14.2 us
    squeeze x14, local copies, waits for them, and re-layouts, pick_micro(): return lax.dynamic_index_in_dim(array, micro_index, 0, keepdims=False)  13.1 us
    another operation x41, local copies, waits for them, and re-layouts  11.5 us
    dot_general x8, matrix products, section_apply(): jnp.dot(normalized, weights_in[2], preferred_element_type=jnp.float32)  10.4 us
  transfers between devices with their start and end apart: 8, of which 6 were waited for; matrix products, arithmetic and copies ran while one was open for 7% of the time, Pallas kernels for 0%

commit v1 on v0

v1 whole, which is shorter than its diff:
```python
import functools
import math

import jax
import jax.numpy as jnp
from jax import lax
from jax.experimental import pallas as pl
from jax.experimental.pallas import tpu as pltpu
from jax.sharding import PartitionSpec as P

BF = jnp.bfloat16
F32 = jnp.float32
MESH = pl.DeviceIdType.MESH
TN = (((1,), (1,)), ((), ()))
NT = (((0,), (0,)), ((), ()))


def dot(a, b):
    return jnp.dot(a, b, preferred_element_type=F32)


def dot_t(a, b):
    return lax.dot_general(a, b, TN, preferred_element_type=F32)


def t_dot(a, b):
    return lax.dot_general(a, b, NT, preferred_element_type=F32)


def one_hot(ids, per_micro, micro_count):
    rows = -(-(4 * micro_count) // 16) * 16
    count = ids.shape[1]
    which = lax.broadcasted_iota(jnp.int32, (rows, count), 0)
    micro = lax.broadcasted_iota(jnp.int32, (rows, count), 1) // per_micro
    return jnp.where(which == ids + 4 * micro, 1.0, 0.0).astype(BF)


def softmax_rows(scores, allowed):
    scores = jnp.where(allowed, scores, -1e30)
    expo = jnp.exp(scores - jnp.max(scores, axis=-1, keepdims=True))
    return expo / jnp.sum(expo, axis=-1, keepdims=True)


def rms_rows(src, dst, scale_ref, step=16):
    for row in range(0, src.shape[0], step):
        x = src[row : row + step, :].astype(F32)
        r = lax.rsqrt(jnp.mean(x * x, axis=-1, keepdims=True) + 1e-06)
        dst[row : row + step, :] = (x * r).astype(BF)
        if scale_ref is not None:
            scale_ref[row : row + step, :] = jnp.broadcast_to(r, (step, 128))


def kernel(
    layers, n, micro_count, parts,
    enc, dec, eid, did, w_in, w_out, cot,
    out_in, out_o,
    inbuf, outbuf, gin, gout, hbuf, mbuf, rbuf, rsbuf, qb, kb, vb, ab, pb, dq, dk, dv, total, *rest,
):
    count = len(parts)
    gs = rest[:count]
    recvs = rest[count : 2 * count]
    fs, fr, bs, br, rs_send, rs_recv = rest[2 * count :]
    bits = n.bit_length() - 1
    half = layers // 2
    te, td = enc.shape[0], dec.shape[0]
    width = enc.shape[1]
    hd = w_in.shape[3]
    scale = 1.0 / math.sqrt(hd)
    deep = layers > 2

    p = lax.axis_index("pipe")
    me = lax.axis_index("dp")
    b = [lax.rem(me // (1 << i), 2) for i in range(bits)]
    partner = [me + (1 - 2 * b[i]) * (1 << i) for i in range(bits)]
    up = lax.rem(p + 1, layers)
    down = lax.rem(p + layers - 1, layers)
    not_first = p > 0
    not_last = p < layers - 1
    is_enc = p < half

    barrier = pltpu.get_barrier_semaphore()
    for q in partner:
        pl.semaphore_signal(barrier, inc=1, device_id=(q, p), device_id_type=MESH)

    @pl.when(not_first)
    def _():
        pl.semaphore_signal(barrier, inc=1, device_id=(me, down), device_id_type=MESH)

    @pl.when(not_last)
    def _():
        pl.semaphore_signal(barrier, inc=1, device_id=(me, up), device_id_type=MESH)

    neighbours = jnp.where(not_first, 1, 0) + jnp.where(not_last, 1, 0)
    pl.semaphore_wait(barrier, bits + neighbours)

    fwd = pltpu.make_async_remote_copy(outbuf, inbuf, fs, fr, device_id=(me, up), device_id_type=MESH)
    bwd = pltpu.make_async_remote_copy(gout, gin, bs, br, device_id=(me, down), device_id_type=MESH)

    mem_enc = inbuf.at[pl.ds(0, te)] if deep else enc
    mem_dec = inbuf.at[pl.ds(0, te)]
    stream = inbuf.at[pl.ds(te, td)] if deep else dec
    g_dec = gin.at[pl.ds(te, td)] if deep else cot
    g_enc = gin.at[pl.ds(0, te)]
    cols = 512

    if deep:

        @pl.when(p == 0)
        def _():
            inbuf[0:te, :] = enc[...]
            inbuf[te : te + td, :] = dec[...]

        @pl.when(p == layers - 1)
        def _():
            gin[0:te, :] = jnp.zeros((te, width), BF)
            gin[te : te + td, :] = cot[...]

    e_hot = one_hot(eid[...], te // micro_count, micro_count)

    def residual_out(src, row0, rows):
        for c in range(0, width, cols):
            y = dot(ab[0:rows, :], w_out[0, :, c : c + cols])
            outbuf[row0 : row0 + rows, c : c + cols] = (
                src[:, c : c + cols].astype(F32) + y
            ).astype(BF)

    def heads(q, k, v, rows, hot):
        qb[0:rows, :] = q
        kb[...] = k
        vb[...] = v
        allowed = t_dot(hot, e_hot) > 0.5
        prob = softmax_rows(dot_t(q, k) * scale, allowed)
        pb[0:rows, :] = prob
        ab[0:rows, :] = dot(prob.astype(BF), v).astype(BF)

    def heads_back(g, rows):
        prob = pb[0:rows, :]
        da = dot_t(g[...], w_out[0]).astype(BF)
        dv[...] = t_dot(prob.astype(BF), da).astype(BF)
        dp = dot_t(da, vb[...]).astype(BF).astype(F32)
        ds = prob * (dp - jnp.sum(prob * dp, axis=-1, keepdims=True)) * scale
        ds = ds.astype(BF)
        dq[0:rows, :] = dot(ds, kb[...]).astype(BF)
        dk[...] = t_dot(ds, qb[0:rows, :]).astype(BF)

    def rms_back(x_ref, pairs, r_ref, add, dst):
        for c in range(0, width, cols):
            dy = None
            for grad, which in pairs:
                term = dot_t(grad[0 : x_ref.shape[0], :], w_in[0, which, c : c + cols, :]).astype(BF)
                dy = term if dy is None else dy + term
            dst[:, c : c + cols] = dy

        step = 16

        def rows_back(i, carry):
            row = pl.ds(pl.multiple_of(i * step, step), step)
            dy = dst[row, :].astype(F32)
            x = x_ref[row, :].astype(F32)
            r = r_ref[row, :][:, 0:1]
            inner = jnp.mean(x * dy, axis=-1, keepdims=True)
            dx = (dy * r - x * (r * r * r * inner)).astype(BF)
            if add is not None:
                dx = dx + add[row, :]
            dst[row, :] = dx
            return carry

        lax.fori_loop(0, x_ref.shape[0] // step, rows_back, 0)

    def grads(left_q, left_kv, left_o, rows):
        for c in range(0, width, cols):
            lq = left_q[0:rows, c : c + cols]
            lkv = left_kv[:, c : c + cols]
            lo = left_o[:, c : c + cols]
            block = jnp.concatenate(
                [
                    t_dot(dq[0:rows, :], lq),
                    t_dot(dk[...], lkv),
                    t_dot(dv[...], lkv),
                    t_dot(ab[0:rows, :], lo),
                ],
                axis=0,
            ).astype(BF)
            size = width // n
            for j in range(cols // size):
                owner = c // size + j
                piece = block[:, j * size : (j + 1) * size]
                flip = [b[i] if not (owner >> i) & 1 else 1 - b[i] for i in range(bits)]
                for g, (lo_row, hi_row, order) in zip(gs, parts):
                    pos = sum(flip[s] * (1 << (bits - 1 - k)) for k, s in enumerate(order))
                    g[pos] = piece[lo_row:hi_row, :]

    @pl.when(not_first)
    def _():
        fwd.wait_recv()

    @pl.when(is_enc)
    def _():
        rms_rows(mem_enc, hbuf, rbuf if deep else None)
        h = hbuf[...]
        q, k, v = [dot(h, w_in[0, i]).astype(BF) for i in range(3)]
        heads(q, k, v, te, e_hot)
        residual_out(mem_enc, 0, te)
        if deep:
            outbuf[te : te + td, :] = inbuf[te : te + td, :]
        fwd.start()

    @pl.when(jnp.logical_not(is_enc))
    def _():
        rms_rows(stream, hbuf.at[pl.ds(0, td)], rsbuf if deep else None)
        rms_rows(mem_dec, mbuf, rbuf)
        q = dot(hbuf[0:td, :], w_in[0, 0]).astype(BF)
        m = mbuf[...]
        k = dot(m, w_in[0, 1]).astype(BF)
        v = dot(m, w_in[0, 2]).astype(BF)
        heads(q, k, v, td, one_hot(did[...], td // micro_count, micro_count))
        if deep:

            @pl.when(not_last)
            def _():
                outbuf[0:te, :] = inbuf[0:te, :]
                residual_out(stream, te, td)
                fwd.start()

    @pl.when(not_last)
    def _():
        bwd.wait_recv()

    @pl.when(jnp.logical_not(is_enc))
    def _():
        heads_back(g_dec, td)
        rms_back(mem_dec, ((dk, 1), (dv, 2)), rbuf, gin.at[pl.ds(0, te)] if deep else None,
                 gout.at[pl.ds(0, te)])
        if deep:
            rms_back(stream, ((dq, 0),), rsbuf, g_dec, gout.at[pl.ds(te, td)])
        bwd.start()
        grads(hbuf, mbuf, g_dec, td)

    @pl.when(is_enc)
    def _():
        heads_back(g_enc, te)
        if deep:

            @pl.when(not_first)
            def _():
                rms_back(mem_enc, ((dq, 0), (dk, 1), (dv, 2)), rbuf, g_enc,
                         gout.at[pl.ds(0, te)])
                gout[te : te + td, :] = gin[te : te + td, :]
                bwd.start()

        grads(hbuf, hbuf, g_enc, te)

    def stage(which, k):
        size = n >> (k + 1)
        return pltpu.make_async_remote_copy(
            gs[which].at[pl.ds(size, size)],
            recvs[which].at[pl.ds(size, size)],
            rs_send.at[which, k],
            rs_recv.at[which, k],
            device_id=(partner[parts[which][2][k]], p),
            device_id_type=MESH,
        )

    for which in range(count):
        stage(which, 0).start()
    for k in range(bits):
        size = n >> (k + 1)
        for which in range(count):
            stage(which, k).wait_recv()
            g, recv = gs[which], recvs[which]
            if k < bits - 1:

                def fold(j, carry):
                    g[j] = (g[j].astype(F32) + recv[size + j].astype(F32)).astype(BF)
                    return carry

                lax.fori_loop(0, size, fold, 0)
                stage(which, k + 1).start()
            else:
                lo_row, hi_row, _ = parts[which]
                total[lo_row:hi_row, :] = g[0].astype(F32) + recv[1].astype(F32)
    for i in range(3):
        out_in[0, i] = total[i * hd : (i + 1) * hd, :].T
    out_o[0] = total[3 * hd : 4 * hd, :]

    for which in range(count):
        for k in range(bits):
            stage(which, k).wait_send()

    @pl.when(not_last)
    def _():
        fwd.wait_send()

    @pl.when(not_first)
    def _():
        bwd.wait_send()


def body(enc_tokens, dec_tokens, enc_segments, dec_segments, proj_in, proj_out, cotangent):
    layers = lax.axis_size("pipe")
    n = lax.axis_size("dp")
    micro_count, te, width = enc_tokens.shape
    td = dec_tokens.shape[1]
    hd = proj_in.shape[3]
    te, td = te * micro_count, td * micro_count
    rows = te + (td if layers > 2 else 0)
    size = width // n
    bits = n.bit_length() - 1
    natural = tuple(range(bits))
    if bits == 4:
        parts = ((0, 192, (0, 1, 2, 3)), (192, 384, (1, 0, 2, 3)), (384, 512, (2, 3, 0, 1)))
    else:
        parts = ((0, 4 * hd, natural),)
    vm = pltpu.VMEM
    slots = [vm((n, hi - lo, size), BF) for lo, hi, _ in parts]
    dma = pltpu.SemaphoreType.DMA
    return pl.pallas_call(
        functools.partial(kernel, layers, n, micro_count, parts),
        out_shape=(
            jax.ShapeDtypeStruct((1, 3, size, hd), F32),
            jax.ShapeDtypeStruct((1, hd, size), F32),
        ),
        in_specs=[pl.BlockSpec(memory_space=pltpu.VMEM)] * 7,
        out_specs=(pl.BlockSpec(memory_space=pltpu.VMEM),) * 2,
        scratch_shapes=[
            vm((rows, width), BF),
            vm((rows, width), BF),
            vm((rows, width), BF),
            vm((rows, width), BF),
            vm((te, width), BF),
            vm((te, width), BF),
            vm((te, 128), F32),
            vm((td, 128), F32),
            vm((te, hd), BF),
            vm((te, hd), BF),
            vm((te, hd), BF),
            vm((te, hd), BF),
            vm((te, te), F32),
            vm((te, hd), BF),
            vm((te, hd), BF),
            vm((te, hd), BF),
            vm((4 * hd, size), F32),
            *slots,
            *slots,
            dma, dma, dma, dma,
            dma((len(parts), bits)),
            dma((len(parts), bits)),
        ],
        compiler_params=pltpu.CompilerParams(
            collective_id=0, has_side_effects=True, vmem_limit_bytes=56 << 20
        ),
    )(
        enc_tokens.reshape(te, width),
        dec_tokens.reshape(td, width),
        enc_segments.reshape(1, te),
        dec_segments.reshape(1, td),
        proj_in,
        proj_out,
        cotangent.reshape(td, width),
    )


def solution(mesh):
    return jax.shard_map(
        body,
        mesh=mesh,
        in_specs=(
            P(None, "dp", None),
            P(None, "dp", None),
            P(None, "dp"),
            P(None, "dp"),
            P("pipe", None, None, None),
            P("pipe", None, None),
            P(None, "dp", None),
        ),
        out_specs=(P("pipe", None, "dp", None), P("pipe", None, "dp")),
        check_vma=False,
    )
```

time: 341 us -> 48.9 us (0.14)
  waiting for transfers between devices: 188 us -> 0 us
  matrix products: 44.4 us -> 0 us
  Pallas kernels: 0 us -> 42.4 us
  other arithmetic: 36.7 us -> 0 us
  local copies, waits for them, and re-layouts: 39.2 us -> 5.68 us
  starting transfers between devices: 14.2 us -> 0 us
  between operations: 14.1 us -> 0.64 us
    reduce_scatter x2 -> x0, waiting for transfers between devices: 162 us -> none  [the longest x1 83.8 us: body(): lax.psum_scatter(totals[0], 'dp', scatter_dimension=1, tiled=True)]
    dot_general x42 -> x0, matrix products: 44.4 us -> none  [the longest x8 10.4 us: section_apply(): jnp.dot(normalized, weights_in[2], preferred_element_type=jnp.float32)]
    pallas_call x0 -> x1, Pallas kernels: none -> 42.4 us  [body(): pl.pallas_call(functools.partial(kernel, layers, n, micro_count, parts),...]
    ppermute x6 -> x0, waiting for transfers between devices: 26.9 us -> none  [shifted(): return lax.ppermute(value, axis, pairs)]
    add x6 -> x0, other arithmetic: 19.9 us -> none  [the longest x3 15.2 us: backward_part(): totals[0] + grad_weights_in]
    squeeze x16 -> x0, local copies, waits for them, and re-layouts: 15.5 us -> none  [the longest x14 13.1 us: pick_micro(): return lax.dynamic_index_in_dim(array, micro_index, 0, keepdims=False)]
    ppermute x6 -> x0, starting transfers between devices: 14.2 us -> none  [shifted(): return lax.ppermute(value, axis, pairs)]
    another operation x41 -> x0, local copies, waits for them, and re-layouts: 11.5 us -> none
  transfers between devices with their start and end apart: 8 -> 0, of which waited for: 6 -> 0; matrix products, arithmetic and copies ran while one was open for 7% -> 0% of each run, Pallas kernels for 0% -> 0%
where the time goes in v1:
time: 48.9 us; the launch traced here: 48.7 us
  Pallas kernels  42.4 us (87%)
  local copies, waits for them, and re-layouts  5.68 us (12%)
  between operations  0.64 us (1%)
    pallas_call x1, Pallas kernels, body(): pl.pallas_call(functools.partial(kernel, layers, n, micro_count, parts),...  42.4 us
    unnamed x2, local copies, waits for them, and re-layouts  3.09 us
    reshape x1, local copies, waits for them, and re-layouts, body(): enc_segments.reshape(1, te)  1.32 us
    reshape x1, local copies, waits for them, and re-layouts, body(): dec_segments.reshape(1, td)  1.27 us

profile of v1, /device:TPU:0, one launch (start us, length us, event | category | flops | bytes accessed | tf_op | source)
XLA Modules:
  0.0 48.7 jit_solution(1302789056300057248)
XLA Ops:
  0.6 1.3 %reshape.22.did = s32[1,64]{1,0:T(1,128)} reshape(s32[2,32]{1,0:T(2,128)} %param.10) | data formatting | bytes 512 | tf_op jit(solution)/shard_map/reshape | solution.py:356
  1.9 1.3 %reshape.21.eid = s32[1,192]{1,0:T(1,128)} reshape(s32[2,96]{1,0:T(2,128)} %param.9) | data formatting | bytes 1536 | tf_op jit(solution)/shard_map/reshape | solution.py:355
  3.2 42.4 %shard_map.86 = (f32[1,3,128,128]{3,2,1,0:T(8,128)}, f32[1,128,128]{2,1,0:T(8,128)}) custom-call(bf16[192,2048]{1,0:T(8,128)(2,1)} %bitcast.3, bf16[64,2048]{1,0:T(8,128)(2,1)} %bitcast.4, s32[1,192]{1,0:T(1,128)} %reshape.21.eid, s32[1,64]{1,0:T(1,128)} %reshape.22.did, bf16[1,3,2048,128]{3,2,1,0:T(8,128)(2,1)} %w_in.1, bf16[1,128,2048]{2,1,0:T(8,128)(2,1)} %w_out.1, ...), custom_call_target="tpu_custom_call" | custom-call | tf_op jit(solution)/shard_map/pallas_call | solution.py:317
  45.6 1.6 %copy.11 = f32[1,3,128,128]{3,2,1,0:T(8,128)} copy(f32[1,3,128,128]{3,2,1,0:T(8,128)} %get-tuple-element.4) | data formatting | bytes 393216
  47.2 1.5 %copy.12 = f32[1,128,128]{2,1,0:T(8,128)} copy(f32[1,128,128]{2,1,0:T(8,128)} %get-tuple-element.5) | data formatting | bytes 131072

commit v2 on v1

--- a/solution.py
+++ b/solution.py
@@ -53,8 +53,8 @@
 def kernel(
     layers, n, micro_count, parts,
     enc, dec, eid, did, w_in, w_out, cot,
-    out_in, out_o,
-    inbuf, outbuf, gin, gout, hbuf, mbuf, rbuf, rsbuf, qb, kb, vb, ab, pb, dq, dk, dv, total, *rest,
+    summed,
+    inbuf, outbuf, gin, gout, hbuf, mbuf, rbuf, rsbuf, qb, kb, vb, ab, pb, dq, dk, dv, eids, dids, *rest,
 ):
     count = len(parts)
     gs = rest[:count]
@@ -93,15 +93,27 @@
     neighbours = jnp.where(not_first, 1, 0) + jnp.where(not_last, 1, 0)
     pl.semaphore_wait(barrier, bits + neighbours)
 
-    fwd = pltpu.make_async_remote_copy(outbuf, inbuf, fs, fr, device_id=(me, up), device_id_type=MESH)
-    bwd = pltpu.make_async_remote_copy(gout, gin, bs, br, device_id=(me, down), device_id_type=MESH)
+    cols = 512
+    chunks = width // cols
+    cut = te // 2
+
+    def fwd(i):
+        part = (slice(None), pl.ds(i * cols, cols))
+        return pltpu.make_async_remote_copy(
+            outbuf.at[part], inbuf.at[part], fs.at[i], fr.at[i], device_id=(me, up), device_id_type=MESH
+        )
+
+    def bwd(i):
+        part = pl.ds(0, cut) if i == 0 else pl.ds(cut, gout.shape[0] - cut)
+        return pltpu.make_async_remote_copy(
+            gout.at[part], gin.at[part], bs.at[i], br.at[i], device_id=(me, down), device_id_type=MESH
+        )
 
     mem_enc = inbuf.at[pl.ds(0, te)] if deep else enc
     mem_dec = inbuf.at[pl.ds(0, te)]
     stream = inbuf.at[pl.ds(te, td)] if deep else dec
     g_dec = gin.at[pl.ds(te, td)] if deep else cot
     g_enc = gin.at[pl.ds(0, te)]
-    cols = 512
 
     if deep:
 
@@ -115,7 +127,11 @@
             gin[0:te, :] = jnp.zeros((te, width), BF)
             gin[te : te + td, :] = cot[...]
 
-    e_hot = one_hot(eid[...], te // micro_count, micro_count)
+    te1, td1 = te // micro_count, td // micro_count
+    for i in range(micro_count):
+        eids[:, i * te1 : (i + 1) * te1] = eid[i : i + 1, :]
+        dids[:, i * td1 : (i + 1) * td1] = did[i : i + 1, :]
+    e_hot = one_hot(eids[...], te1, micro_count)
 
     def residual_out(src, row0, rows):
         for c in range(0, width, cols):
@@ -123,6 +139,7 @@
             outbuf[row0 : row0 + rows, c : c + cols] = (
                 src[:, c : c + cols].astype(F32) + y
             ).astype(BF)
+            fwd(c // cols).start()
 
     def heads(q, k, v, rows, hot):
         qb[0:rows, :] = q
@@ -143,7 +160,7 @@
         dq[0:rows, :] = dot(ds, kb[...]).astype(BF)
         dk[...] = t_dot(ds, qb[0:rows, :]).astype(BF)
 
-    def rms_back(x_ref, pairs, r_ref, add, dst):
+    def rms_back(x_ref, pairs, r_ref, add, dst, early=True):
         for c in range(0, width, cols):
             dy = None
             for grad, which in pairs:
@@ -165,90 +182,13 @@
             dst[row, :] = dx
             return carry
 
-        lax.fori_loop(0, x_ref.shape[0] // step, rows_back, 0)
-
-    def grads(left_q, left_kv, left_o, rows):
-        for c in range(0, width, cols):
-            lq = left_q[0:rows, c : c + cols]
-            lkv = left_kv[:, c : c + cols]
-            lo = left_o[:, c : c + cols]
-            block = jnp.concatenate(
-                [
-                    t_dot(dq[0:rows, :], lq),
-                    t_dot(dk[...], lkv),
-                    t_dot(dv[...], lkv),
-                    t_dot(ab[0:rows, :], lo),
-                ],
-                axis=0,
-            ).astype(BF)
-            size = width // n
-            for j in range(cols // size):
-                owner = c // size + j
-                piece = block[:, j * size : (j + 1) * size]
-                flip = [b[i] if not (owner >> i) & 1 else 1 - b[i] for i in range(bits)]
-                for g, (lo_row, hi_row, order) in zip(gs, parts):
-                    pos = sum(flip[s] * (1 << (bits - 1 - k)) for k, s in enumerate(order))
-                    g[pos] = piece[lo_row:hi_row, :]
-
-    @pl.when(not_first)
-    def _():
-        fwd.wait_recv()
-
-    @pl.when(is_enc)
-    def _():
-        rms_rows(mem_enc, hbuf, rbuf if deep else None)
-        h = hbuf[...]
-        q, k, v = [dot(h, w_in[0, i]).astype(BF) for i in range(3)]
-        heads(q, k, v, te, e_hot)
-        residual_out(mem_enc, 0, te)
-        if deep:
-            outbuf[te : te + td, :] = inbuf[te : te + td, :]
-        fwd.start()
-
-    @pl.when(jnp.logical_not(is_enc))
-    def _():
-        rms_rows(stream, hbuf.at[pl.ds(0, td)], rsbuf if deep else None)
-        rms_rows(mem_dec, mbuf, rbuf)
-        q = dot(hbuf[0:td, :], w_in[0, 0]).astype(BF)
-        m = mbuf[...]
-        k = dot(m, w_in[0, 1]).astype(BF)
-        v = dot(m, w_in[0, 2]).astype(BF)
-        heads(q, k, v, td, one_hot(did[...], td // micro_count, micro_count))
-        if deep:
-
-            @pl.when(not_last)
-            def _():
-                outbuf[0:te, :] = inbuf[0:te, :]
-                residual_out(stream, te, td)
-                fwd.start()
-
-    @pl.when(not_last)
-    def _():
-        bwd.wait_recv()
-
-    @pl.when(jnp.logical_not(is_enc))
-    def _():
-        heads_back(g_dec, td)
-        rms_back(mem_dec, ((dk, 1), (dv, 2)), rbuf, gin.at[pl.ds(0, te)] if deep else None,
-                 gout.at[pl.ds(0, te)])
-        if deep:
-            rms_back(stream, ((dq, 0),), rsbuf, g_dec, gout.at[pl.ds(te, td)])
-        bwd.start()
-        grads(hbuf, mbuf, g_dec, td)
-
-    @pl.when(is_enc)
-    def _():
-        heads_back(g_enc, te)
-        if deep:
-
-            @pl.when(not_first)
-            def _():
-                rms_back(mem_enc, ((dq, 0), (dk, 1), (dv, 2)), rbuf, g_enc,
-                         gout.at[pl.ds(0, te)])
-                gout[te : te + td, :] = gin[te : te + td, :]
-                bwd.start()
-
-        grads(hbuf, hbuf, g_enc, te)
+        steps = x_ref.shape[0] // step
+        if early:
+            lax.fori_loop(0, steps // 2, rows_back, 0)
+            bwd(0).start()
+            lax.fori_loop(steps // 2, steps, rows_back, 0)
+        else:
+            lax.fori_loop(0, steps, rows_back, 0)
 
     def stage(which, k):
         size = n >> (k + 1)
@@ -261,8 +201,109 @@
             device_id_type=MESH,
         )
 
-    for which in range(count):
-        stage(which, 0).start()
+    size = width // n
+
+    def spread(block, c, base, chosen):
+        for j in range(cols // size):
+            owner = c // size + j
+            piece = block[:, j * size : (j + 1) * size]
+            flip = [b[i] if not (owner >> i) & 1 else 1 - b[i] for i in range(bits)]
+            for which in chosen:
+                lo_row, hi_row, order = parts[which]
+                pos = sum(flip[s] * (1 << (bits - 1 - k)) for k, s in enumerate(order))
+                gs[which][pos] = piece[lo_row - base : hi_row - base, :]
+
+    out_parts = [i for i in range(count) if parts[i][0] >= 3 * hd]
+    in_parts = [i for i in range(count) if parts[i][0] < 3 * hd]
+
+    def out_grads(left_o, rows):
+        for c in range(0, width, cols):
+            block = t_dot(ab[0:rows, :], left_o[:, c : c + cols]).astype(BF)
+            spread(block, c, 3 * hd, out_parts)
+        for which in out_parts:
+            stage(which, 0).start()
+
+    def grads(left_q, left_kv, rows):
+        for c in range(0, width, cols):
+            lq = left_q[0:rows, c : c + cols]
+            lkv = left_kv[:, c : c + cols]
+            block = jnp.concatenate(
+                [t_dot(dq[0:rows, :], lq), t_dot(dk[...], lkv), t_dot(dv[...], lkv)], axis=0
+            ).astype(BF)
+            spread(block, c, 0, in_parts)
+        for which in in_parts:
+            stage(which, 0).start()
+
+    def decoder_query():
+        rms_rows(stream, hbuf.at[pl.ds(0, td)], rsbuf if deep else None)
+        qb[0:td, :] = dot(hbuf[0:td, :], w_in[0, 0]).astype(BF)
+
+    if not deep:
+        pl.when(jnp.logical_not(is_enc))(decoder_query)
+
+    @pl.when(not_first)
+    def _():
+        for i in range(chunks):
+            fwd(i).wait_recv()
+
+    @pl.when(is_enc)
+    def _():
+        rms_rows(mem_enc, hbuf, rbuf if deep else None)
+        h = hbuf[...]
+        q, k, v = [dot(h, w_in[0, i]).astype(BF) for i in range(3)]
+        heads(q, k, v, te, e_hot)
+        if deep:
+            outbuf[te : te + td, :] = inbuf[te : te + td, :]
+        residual_out(mem_enc, 0, te)
+
+    @pl.when(jnp.logical_not(is_enc))
+    def _():
+        if deep:
+            decoder_query()
+        rms_rows(mem_dec, mbuf, rbuf)
+        q = qb[0:td, :]
+        m = mbuf[...]
+        k = dot(m, w_in[0, 1]).astype(BF)
+        v = dot(m, w_in[0, 2]).astype(BF)
+        heads(q, k, v, td, one_hot(dids[...], td1, micro_count))
+        if deep:
+
+            @pl.when(not_last)
+            def _():
+                outbuf[0:te, :] = inbuf[0:te, :]
+                residual_out(stream, te, td)
+
+    @pl.when(not_last)
+    def _():
+        for i in range(2):
+            bwd(i).wait_recv()
+
+    @pl.when(jnp.logical_not(is_enc))
+    def _():
+        heads_back(g_dec, td)
+        rms_back(mem_dec, ((dk, 1), (dv, 2)), rbuf, gin.at[pl.ds(0, te)] if deep else None,
+                 gout.at[pl.ds(0, te)])
+        if deep:
+            rms_back(stream, ((dq, 0),), rsbuf, g_dec, gout.at[pl.ds(te, td)], False)
+        bwd(1).start()
+        out_grads(g_dec, td)
+        grads(hbuf, mbuf, td)
+
+    @pl.when(is_enc)
+    def _():
+        out_grads(g_enc, te)
+        heads_back(g_enc, te)
+        if deep:
+
+            @pl.when(not_first)
+            def _():
+                rms_back(mem_enc, ((dq, 0), (dk, 1), (dv, 2)), rbuf, g_enc,
+                         gout.at[pl.ds(0, te)])
+                gout[te : te + td, :] = gin[te : te + td, :]
+                bwd(1).start()
+
+        grads(hbuf, hbuf, te)
+
     for k in range(bits):
         size = n >> (k + 1)
         for which in range(count):
@@ -278,22 +319,27 @@
                 stage(which, k + 1).start()
             else:
                 lo_row, hi_row, _ = parts[which]
-                total[lo_row:hi_row, :] = g[0].astype(F32) + recv[1].astype(F32)
-    for i in range(3):
-        out_in[0, i] = total[i * hd : (i + 1) * hd, :].T
-    out_o[0] = total[3 * hd : 4 * hd, :]
-
+                summed[lo_row:hi_row, :] = g[0].astype(F32) + recv[1].astype(F32)
     for which in range(count):
         for k in range(bits):
             stage(which, k).wait_send()
 
     @pl.when(not_last)
     def _():
-        fwd.wait_send()
+        for i in range(chunks):
+            fwd(i).wait_send()
 
     @pl.when(not_first)
     def _():
-        bwd.wait_send()
+        for i in range(2):
+            bwd(i).wait_send()
+
+
+def place(summed, out_in, out_o):
+    hd = out_in.shape[3]
+    for i in range(3):
+        out_in[0, i] = summed[i * hd : (i + 1) * hd, :].T
+    out_o[0] = summed[3 * hd : 4 * hd, :]
 
 
 def body(enc_tokens, dec_tokens, enc_segments, dec_segments, proj_in, proj_out, cotangent):
@@ -308,20 +354,21 @@
     bits = n.bit_length() - 1
     natural = tuple(range(bits))
     if bits == 4:
-        parts = ((0, 192, (0, 1, 2, 3)), (192, 384, (1, 0, 2, 3)), (384, 512, (2, 3, 0, 1)))
+        xyz, yxz, zxy = (0, 1, 2, 3), (1, 0, 2, 3), (2, 3, 0, 1)
+        parts = (
+            (384, 448, zxy), (448, 512, zxy), (0, 96, xyz),
+            (192, 288, yxz), (96, 192, xyz), (288, 384, yxz),
+        )
     else:
-        parts = ((0, 4 * hd, natural),)
+        parts = ((3 * hd, 4 * hd, natural), (0, 3 * hd, natural))
     vm = pltpu.VMEM
     slots = [vm((n, hi - lo, size), BF) for lo, hi, _ in parts]
     dma = pltpu.SemaphoreType.DMA
-    return pl.pallas_call(
+    summed = pl.pallas_call(
         functools.partial(kernel, layers, n, micro_count, parts),
-        out_shape=(
-            jax.ShapeDtypeStruct((1, 3, size, hd), F32),
-            jax.ShapeDtypeStruct((1, hd, size), F32),
-        ),
+        out_shape=jax.ShapeDtypeStruct((4 * hd, size), F32),
         in_specs=[pl.BlockSpec(memory_space=pltpu.VMEM)] * 7,
-        out_specs=(pl.BlockSpec(memory_space=pltpu.VMEM),) * 2,
+        out_specs=pl.BlockSpec(memory_space=pltpu.VMEM),
         scratch_shapes=[
             vm((rows, width), BF),
             vm((rows, width), BF),
@@ -339,10 +386,11 @@
             vm((te, hd), BF),
             vm((te, hd), BF),
             vm((te, hd), BF),
-            vm((4 * hd, size), F32),
+            vm((1, te), jnp.int32),
+            vm((1, td), jnp.int32),
             *slots,
             *slots,
-            dma, dma, dma, dma,
+            dma((width // 512,)), dma((width // 512,)), dma((2,)), dma((2,)),
             dma((len(parts), bits)),
             dma((len(parts), bits)),
         ],
@@ -352,12 +400,21 @@
     )(
         enc_tokens.reshape(te, width),
         dec_tokens.reshape(td, width),
-        enc_segments.reshape(1, te),
-        dec_segments.reshape(1, td),
+        enc_segments,
+        dec_segments,
         proj_in,
         proj_out,
         cotangent.reshape(td, width),
     )
+    return pl.pallas_call(
+        place,
+        out_shape=(
+            jax.ShapeDtypeStruct((1, 3, size, hd), F32),
+            jax.ShapeDtypeStruct((1, hd, size), F32),
+        ),
+        in_specs=[pl.BlockSpec(memory_space=pltpu.VMEM)],
+        out_specs=(pl.BlockSpec(memory_space=pltpu.VMEM),) * 2,
+    )(summed)
 
 
 def solution(mesh):

time: 48.9 us -> 43.4 us (0.89)
  local copies, waits for them, and re-layouts: 5.68 us -> 0 us
    unnamed x2 -> x0, local copies, waits for them, and re-layouts: 3.09 us -> none
    reshape x2 -> x0, local copies, waits for them, and re-layouts: 2.59 us -> none  [the longest x1 1.32 us: body(): enc_segments.reshape(1, te)]
    pallas_call x0 -> x1, Pallas kernels: none -> 1.76 us  [body(): pl.pallas_call(place, out_shape=(jax.ShapeDtypeStruct((1, 3, size, hd), F...]
    pallas_call x1, Pallas kernels: 42.4 us -> 40.8 us  [body(): pl.pallas_call(functools.partial(kernel, layers, n, micro_count, parts),...]
where the time goes in v2:
time: 43.4 us; the launch traced here: 43.2 us
  Pallas kernels  42.5 us (98%)
  between operations  0.64 us (1%)
    pallas_call x1, Pallas kernels, body(): pl.pallas_call(functools.partial(kernel, layers, n, micro_count, parts),...  40.8 us
    pallas_call x1, Pallas kernels, body(): pl.pallas_call(place, out_shape=(jax.ShapeDtypeStruct((1, 3, size, hd), F...  1.76 us

profile of v2, /device:TPU:0, one launch (start us, length us, event | category | flops | bytes accessed | tf_op | source)
XLA Modules:
  0.0 43.2 jit_solution(1770845767079016612)
XLA Ops:
  0.6 40.8 %shard_map.86.summed = f32[512,128]{1,0:T(8,128)} custom-call(bf16[192,2048]{1,0:T(8,128)(2,1)} %bitcast.3, bf16[64,2048]{1,0:T(8,128)(2,1)} %bitcast.4, s32[2,96]{1,0:T(2,128)} %eid.1, s32[2,32]{1,0:T(2,128)} %did.1, bf16[1,3,2048,128]{3,2,1,0:T(8,128)(2,1)} %w_in.1, bf16[1,128,2048]{2,1,0:T(8,128)(2,1)} %w_out.1, bf16[64,2048]{1,0:T(8,128)(2,1)} %bitcast.5), custom_call_target="tpu_custom_call" | custom-call | tf_op jit(solution)/shard_map/pallas_call | solution.py:367
  41.4 1.8 %shard_map.87 = (f32[1,3,128,128]{3,2,1,0:T(8,128)}, f32[1,128,128]{2,1,0:T(8,128)}) custom-call(f32[512,128]{1,0:T(8,128)} %shard_map.86.summed), custom_call_target="tpu_custom_call" | custom-call | tf_op jit(solution)/shard_map/pallas_call | solution.py:409

commit v3 on v2

--- a/solution.py
+++ b/solution.py
@@ -90,9 +90,6 @@
     def _():
         pl.semaphore_signal(barrier, inc=1, device_id=(me, up), device_id_type=MESH)
 
-    neighbours = jnp.where(not_first, 1, 0) + jnp.where(not_last, 1, 0)
-    pl.semaphore_wait(barrier, bits + neighbours)
-
     cols = 512
     chunks = width // cols
     cut = te // 2
@@ -238,21 +235,28 @@
         rms_rows(stream, hbuf.at[pl.ds(0, td)], rsbuf if deep else None)
         qb[0:td, :] = dot(hbuf[0:td, :], w_in[0, 0]).astype(BF)
 
-    if not deep:
-        pl.when(jnp.logical_not(is_enc))(decoder_query)
-
-    @pl.when(not_first)
-    def _():
-        for i in range(chunks):
-            fwd(i).wait_recv()
-
-    @pl.when(is_enc)
-    def _():
+    def encoder_heads():
         rms_rows(mem_enc, hbuf, rbuf if deep else None)
         h = hbuf[...]
         q, k, v = [dot(h, w_in[0, i]).astype(BF) for i in range(3)]
         heads(q, k, v, te, e_hot)
+
+    if not deep:
+        pl.when(jnp.logical_not(is_enc))(decoder_query)
+        pl.when(is_enc)(encoder_heads)
+
+    neighbours = jnp.where(not_first, 1, 0) + jnp.where(not_last, 1, 0)
+    pl.semaphore_wait(barrier, bits + neighbours)
+
+    @pl.when(not_first)
+    def _():
+        for i in range(chunks):
+            fwd(i).wait_recv()
+
+    @pl.when(is_enc)
+    def _():
         if deep:
+            encoder_heads()
             outbuf[te : te + td, :] = inbuf[te : te + td, :]
         residual_out(mem_enc, 0, te)
 

time: 43.4 us -> 43.4 us (level)
  no operation moved by 1% of the time
where the time goes in v3:
time: 43.4 us; the launch traced here: 43.2 us
  Pallas kernels  42.6 us (98%)
  between operations  0.64 us (1%)
    pallas_call x1, Pallas kernels, body(): pl.pallas_call(functools.partial(kernel, layers, n, micro_count, parts),...  40.8 us
    pallas_call x1, Pallas kernels, body(): pl.pallas_call(place, out_shape=(jax.ShapeDtypeStruct((1, 3, size, hd), F...  1.76 us

profile of v3, /device:TPU:0, one launch (start us, length us, event | category | flops | bytes accessed | tf_op | source)
XLA Modules:
  0.0 43.2 jit_solution(7395074601437440079)
XLA Ops:
  0.6 40.8 %shard_map.86.summed = f32[512,128]{1,0:T(8,128)} custom-call(bf16[192,2048]{1,0:T(8,128)(2,1)} %bitcast.3, bf16[64,2048]{1,0:T(8,128)(2,1)} %bitcast.4, s32[2,96]{1,0:T(2,128)} %eid.1, s32[2,32]{1,0:T(2,128)} %did.1, bf16[1,3,2048,128]{3,2,1,0:T(8,128)(2,1)} %w_in.1, bf16[1,128,2048]{2,1,0:T(8,128)(2,1)} %w_out.1, bf16[64,2048]{1,0:T(8,128)(2,1)} %bitcast.5), custom_call_target="tpu_custom_call" | custom-call | tf_op jit(solution)/shard_map/pallas_call | solution.py:371
  41.4 1.8 %shard_map.87 = (f32[1,3,128,128]{3,2,1,0:T(8,128)}, f32[1,128,128]{2,1,0:T(8,128)}) custom-call(f32[512,128]{1,0:T(8,128)} %shard_map.86.summed), custom_call_target="tpu_custom_call" | custom-call | tf_op jit(solution)/shard_map/pallas_call | solution.py:413

commit v4 on v2

--- a/solution.py
+++ b/solution.py
@@ -54,7 +54,7 @@
     layers, n, micro_count, parts,
     enc, dec, eid, did, w_in, w_out, cot,
     summed,
-    inbuf, outbuf, gin, gout, hbuf, mbuf, rbuf, rsbuf, qb, kb, vb, ab, pb, dq, dk, dv, eids, dids, *rest,
+    inbuf, outbuf, gin, gout, hbuf, mbuf, rbuf, rsbuf, qb, kb, vb, ab, pb, dq, dk, dv, eids, dids, w_got, a_got, *rest,
 ):
     count = len(parts)
     gs = rest[:count]
@@ -109,6 +109,18 @@
             gout.at[part], gin.at[part], bs.at[i], br.at[i], device_id=(me, down), device_id_type=MESH
         )
 
+    def small(i):
+        src, dst = ((w_out.at[0], w_got), (ab, a_got))[i]
+        return pltpu.make_async_remote_copy(
+            src, dst, fs.at[i], fr.at[i], device_id=(me, up), device_id_type=MESH
+        )
+
+    if not deep:
+
+        @pl.when(is_enc)
+        def _():
+            small(0).start()
+
     mem_enc = inbuf.at[pl.ds(0, te)] if deep else enc
     mem_dec = inbuf.at[pl.ds(0, te)]
     stream = inbuf.at[pl.ds(te, td)] if deep else dec
@@ -243,8 +255,15 @@
 
     @pl.when(not_first)
     def _():
-        for i in range(chunks):
-            fwd(i).wait_recv()
+        if deep:
+            for i in range(chunks):
+                fwd(i).wait_recv()
+        else:
+            small(0).wait_recv()
+            small(1).wait_recv()
+            for c in range(0, width, cols):
+                y = dot(a_got[...], w_got[:, c : c + cols])
+                inbuf[:, c : c + cols] = (enc[:, c : c + cols].astype(F32) + y).astype(BF)
 
     @pl.when(is_enc)
     def _():
@@ -254,7 +273,9 @@
         heads(q, k, v, te, e_hot)
         if deep:
             outbuf[te : te + td, :] = inbuf[te : te + td, :]
-        residual_out(mem_enc, 0, te)
+            residual_out(mem_enc, 0, te)
+        else:
+            small(1).start()
 
     @pl.when(jnp.logical_not(is_enc))
     def _():
@@ -326,8 +347,12 @@
 
     @pl.when(not_last)
     def _():
-        for i in range(chunks):
-            fwd(i).wait_send()
+        if deep:
+            for i in range(chunks):
+                fwd(i).wait_send()
+        else:
+            small(0).wait_send()
+            small(1).wait_send()
 
     @pl.when(not_first)
     def _():
@@ -388,6 +413,8 @@
             vm((te, hd), BF),
             vm((1, te), jnp.int32),
             vm((1, td), jnp.int32),
+            vm((hd, width), BF),
+            vm((te, hd), BF),
             *slots,
             *slots,
             dma((width // 512,)), dma((width // 512,)), dma((2,)), dma((2,)),

time: 43.4 us -> 42.5 us (0.979)
  Pallas kernels: 42.5 us -> 41.7 us
    pallas_call x1, Pallas kernels: 40.8 us -> 40 us  [body(): pl.pallas_call(functools.partial(kernel, layers, n, micro_count, parts),...]
where the time goes in v4:
time: 42.5 us; the launch traced here: 42.4 us
  Pallas kernels  41.7 us (98%)
  between operations  0.64 us (2%)
    pallas_call x1, Pallas kernels, body(): pl.pallas_call(functools.partial(kernel, layers, n, micro_count, parts),...  40 us
    pallas_call x1, Pallas kernels, body(): pl.pallas_call(place, out_shape=(jax.ShapeDtypeStruct((1, 3, size, hd), F...  1.76 us

profile of v4, /device:TPU:0, one launch (start us, length us, event | category | flops | bytes accessed | tf_op | source)
XLA Modules:
  0.0 42.4 jit_solution(7310455812980236950)
XLA Ops:
  0.6 40.0 %shard_map.86.summed = f32[512,128]{1,0:T(8,128)} custom-call(bf16[192,2048]{1,0:T(8,128)(2,1)} %bitcast.3, bf16[64,2048]{1,0:T(8,128)(2,1)} %bitcast.4, s32[2,96]{1,0:T(2,128)} %eid.1, s32[2,32]{1,0:T(2,128)} %did.1, bf16[1,3,2048,128]{3,2,1,0:T(8,128)(2,1)} %w_in.1, bf16[1,128,2048]{2,1,0:T(8,128)(2,1)} %w_out.1, bf16[64,2048]{1,0:T(8,128)(2,1)} %bitcast.5), custom_call_target="tpu_custom_call" | custom-call | tf_op jit(solution)/shard_map/pallas_call | solution.py:392
  40.6 1.8 %shard_map.87 = (f32[1,3,128,128]{3,2,1,0:T(8,128)}, f32[1,128,128]{2,1,0:T(8,128)}) custom-call(f32[512,128]{1,0:T(8,128)} %shard_map.86.summed), custom_call_target="tpu_custom_call" | custom-call | tf_op jit(solution)/shard_map/pallas_call | solution.py:436
